TPU v7x, 32 devices: a whole 2x2x4 slice. The times are simulated.
32 devices in a mesh: ctx: 16 (over z, y, core), head: 2 (over x).
Axes of the slice: x: 2, y: 2, z: 4, core: 2. Of those that a mesh axis runs over, the one named last changes fastest.
Arguments:
- queries: bfloat16 [2048, 2048], P('ctx', 'head'), may hold values from -8 to 8, as said below
- key_codes: bfloat16 [2, 2048, 128], P(None, 'ctx'), may hold values from -6 to 6
- key_scale: float32 [2, 2048], P(None, 'ctx'), may hold values from 0.5 to 2
- value_codes: bfloat16 [2, 2048, 128], P(None, 'ctx'), may hold values from -6 to 6
- value_scale: float32 [2, 2048], P(None, 'ctx'), may hold values from 0.5 to 2
- evict_flags: int32 [2, 2048], P(None, 'ctx'), may hold values from 0 to 1, as said below
- out_forward: bfloat16 [2048, 2048], P('ctx', 'head'), may hold values from -12 to 12, as said below
- grad_output: bfloat16 [2048, 2048], P('ctx', 'head'), may hold values from -6 to 6
- log_norm: float32 [16, 2048], P('head', 'ctx'), as said below
Outputs:
- grad_queries: bfloat16 [2048, 2048], P('ctx', 'head')
- grad_keys: bfloat16 [2, 2048, 128], P(None, 'ctx')
- grad_values: bfloat16 [2, 2048, 128], P(None, 'ctx')
Inputs may be any that keep to these rules, and one draw needn't show every extreme that they name: queries hold bfloat16 values. `evict_flags`: each token and key and value head is evicted independently with probability one half. log_norm is the log of the sum of exp(c * scores) over the visible keys of each query, from the same queries, keys and flags. out_forward is the forward attention output of the same inputs, rounded to bfloat16.
All inputs are finite; a program needn't handle non-finite values.
Results may differ from a plain program's by a relative error of at most 0.0033.
The roundings to bfloat16 on the way count: a program that leaves them out, or rounds other values in their place, can miss the bound.
Values may be sent and summed in bfloat16 or wider, within the bound.
A program may use at most 64 MiB of HBM per device.

v0:
```python
import math

import jax
import jax.numpy as jnp
from jax import lax
from jax.sharding import PartitionSpec as P

ASKER_PROJ_NUM = 16
KEY_VALUE_HEADS = 2
DELAY = 256


def swapped(block, axis, stride):
    count = lax.axis_size(axis)
    route = []
    for low in range(count):
        high = low | 1 << stride
        if high != low and high < count:
            route += [(low, high), (high, low)]
    return lax.ppermute(block, axis, route)


def token_position(rows, tok_dev, ctx_count):
    device_row = rows // tok_dev
    within = rows % tok_dev
    half = tok_dev // 2
    return jnp.where(
        within < half,
        device_row * half + within,
        (2 * ctx_count - 1 - device_row) * half + within - half,
    )


def block_terms(
    query_block_rows,
    gradient_block,
    norm_blk,
    delta_blk,
    query_pos,
    key_block_rows,
    value_block_rows,
    evict_blk,
    key_pos,
):
    softmax_factor = query_block_rows.shape[2] ** (-0.5)
    score_matrix = (
        jnp.einsum(
            "vjt,qt->jvq", query_block_rows, key_block_rows, preferred_element_type=jnp.float32
        )
        * softmax_factor
    )
    distance = query_pos[:, None] - key_pos[None, :]
    visible = (distance >= 0) & ((evict_blk[None, :] == 0) | (distance < DELAY))
    attention_weights = jnp.where(
        visible[None], jnp.exp(score_matrix - norm_blk.T[:, :, None]), 0.0
    )
    weight_gradient = jnp.einsum(
        "vjt,qt->jvq", gradient_block, value_block_rows, preferred_element_type=jnp.float32
    )
    score_gradient = (
        softmax_factor * attention_weights * (weight_gradient - delta_blk.T[:, :, None])
    )
    return (attention_weights.astype(jnp.bfloat16), score_gradient.astype(jnp.bfloat16))


def query_grads(
    cumulative_sums,
    query_heads,
    grad_heads,
    norm_rows,
    row_delta,
    own_pos,
    key_piece,
    value_piece,
    evict_piece,
    tok_dev,
    ctx_count,
):
    piece_len = key_piece.shape[0]
    step_len = math.gcd(piece_len, 512)

    def query_sub_block(step_index, running):
        within = step_index * step_len
        key_block_rows = lax.dynamic_slice_in_dim(key_piece, within, step_len, 0)
        value_block_rows = lax.dynamic_slice_in_dim(value_piece, within, step_len, 0)
        evict_blk = lax.dynamic_slice_in_dim(evict_piece, within, step_len, 0)
        key_pos = token_position(within + jnp.arange(step_len, dtype=jnp.int32), tok_dev, ctx_count)
        unused, score_gradient = block_terms(
            query_heads,
            grad_heads,
            norm_rows,
            row_delta,
            own_pos,
            key_block_rows,
            value_block_rows,
            evict_blk,
            key_pos,
        )
        return running + jnp.einsum(
            "gzs,sp->zgp", score_gradient, key_block_rows, preferred_element_type=jnp.float32
        )

    return lax.fori_loop(0, piece_len // step_len, query_sub_block, cumulative_sums)


def key_grads(
    cumulative_sums,
    key_rows,
    value_rows,
    evicted,
    own_pos,
    query_piece,
    grad_piece,
    norm_piece,
    delta_piece,
    tok_dev,
    ctx_count,
):
    piece_len = query_piece.shape[0]
    head_count = norm_piece.shape[1]
    head_width = key_rows.shape[1]
    step_len = math.gcd(piece_len, 512)

    def key_sub_block(step_index, running):
        within = step_index * step_len
        query_block_rows = lax.dynamic_slice_in_dim(query_piece, within, step_len, 0).reshape(
            step_len, head_count, head_width
        )
        gradient_block = lax.dynamic_slice_in_dim(grad_piece, within, step_len, 0).reshape(
            step_len, head_count, head_width
        )
        norm_blk = lax.dynamic_slice_in_dim(norm_piece, within, step_len, 0)
        delta_blk = lax.dynamic_slice_in_dim(delta_piece, within, step_len, 0)
        query_pos = token_position(
            within + jnp.arange(step_len, dtype=jnp.int32), tok_dev, ctx_count
        )
        attention_weights, score_gradient = block_terms(
            query_block_rows,
            gradient_block,
            norm_blk,
            delta_blk,
            query_pos,
            key_rows,
            value_rows,
            evicted,
            own_pos,
        )
        key_portion = jnp.einsum(
            "lnf,nlb->fb", score_gradient, query_block_rows, preferred_element_type=jnp.float32
        )
        value_portion = jnp.einsum(
            "lnf,nlb->fb", attention_weights, gradient_block, preferred_element_type=jnp.float32
        )
        return (running[0] + key_portion, running[1] + value_portion)

    return lax.fori_loop(0, piece_len // step_len, key_sub_block, cumulative_sums)


def local(
    queries,
    key_codes,
    key_scale,
    value_codes,
    value_scale,
    evict_flags,
    out_forward,
    grad_output,
    log_norm,
):
    row_count = queries.shape[0]
    head_count = log_norm.shape[0]
    head_width = key_codes.shape[2]
    ctx_count = lax.axis_size("ctx")
    group_width = ASKER_PROJ_NUM // KEY_VALUE_HEADS
    kv_index = lax.axis_index("head") * head_count // group_width
    own_pos = token_position(
        lax.axis_index("ctx") * row_count + jnp.arange(row_count, dtype=jnp.int32),
        row_count,
        ctx_count,
    )
    own_keys = lax.dynamic_index_in_dim(key_codes, kv_index, 0, keepdims=False)
    own_key_scale = lax.dynamic_index_in_dim(key_scale, kv_index, 0, keepdims=False)
    key_rows = (own_keys.astype(jnp.float32) * own_key_scale[:, None]).astype(jnp.bfloat16)
    own_values = lax.dynamic_index_in_dim(value_codes, kv_index, 0, keepdims=False)
    own_value_scale = lax.dynamic_index_in_dim(value_scale, kv_index, 0, keepdims=False)
    value_rows = (own_values.astype(jnp.float32) * own_value_scale[:, None]).astype(jnp.bfloat16)
    evicted = lax.dynamic_index_in_dim(evict_flags, kv_index, 0, keepdims=False)
    query_heads = queries.reshape(row_count, head_count, head_width)
    grad_heads = grad_output.reshape(row_count, head_count, head_width)
    out_heads = out_forward.reshape(row_count, head_count, head_width)
    row_delta = jnp.sum(grad_heads.astype(jnp.float32) * out_heads.astype(jnp.float32), axis=2)
    norm_rows = log_norm.T
    empty_query = jnp.zeros((row_count, head_count, head_width), jnp.float32)
    empty_key = jnp.zeros((row_count, head_width), jnp.float32)
    key_piece = lax.all_gather(key_rows, "ctx", axis=0, tiled=True)
    value_piece = lax.all_gather(value_rows, "ctx", axis=0, tiled=True)
    evict_piece = lax.all_gather(evicted, "ctx", axis=0, tiled=True)
    asker_derivative = query_grads(
        empty_query,
        query_heads,
        grad_heads,
        norm_rows,
        row_delta,
        own_pos,
        key_piece,
        value_piece,
        evict_piece,
        row_count,
        ctx_count,
    )
    query_piece = lax.all_gather(queries.astype(jnp.float32), "ctx", axis=0, tiled=True).astype(
        jnp.bfloat16
    )
    grad_piece = lax.all_gather(grad_output.astype(jnp.float32), "ctx", axis=0, tiled=True).astype(
        jnp.bfloat16
    )
    norm_piece = lax.all_gather(norm_rows, "ctx", axis=0, tiled=True)
    delta_piece = lax.all_gather(row_delta, "ctx", axis=0, tiled=True)
    key_grad, value_grad = key_grads(
        (empty_key, empty_key),
        key_rows,
        value_rows,
        evicted,
        own_pos,
        query_piece,
        grad_piece,
        norm_piece,
        delta_piece,
        row_count,
        ctx_count,
    )
    per_group = lax.axis_size("head") // KEY_VALUE_HEADS
    group_bits = per_group.bit_length() - 1
    key_total, value_total = (key_grad, value_grad)
    for bit in range(group_bits):
        other_key, other_value = swapped((key_total, value_total), "head", bit)
        key_total = key_total + other_key
        value_total = value_total + other_value
    key_mine = key_total.astype(jnp.bfloat16)
    value_mine = value_total.astype(jnp.bfloat16)
    key_other, value_other = swapped((key_mine, value_mine), "head", group_bits)
    first = kv_index == 0
    key_sum = jnp.where(first, jnp.stack([key_mine, key_other]), jnp.stack([key_other, key_mine]))
    value_sum = jnp.where(
        first, jnp.stack([value_mine, value_other]), jnp.stack([value_other, value_mine])
    )
    grad_queries = asker_derivative.reshape(row_count, head_count * head_width).astype(jnp.bfloat16)
    return (grad_queries, key_sum, value_sum)


def solution(mesh):
    in_specs = (
        P("ctx", "head"),
        P(None, "ctx", None),
        P(None, "ctx"),
        P(None, "ctx", None),
        P(None, "ctx"),
        P(None, "ctx"),
        P("ctx", "head"),
        P("ctx", "head"),
        P("head", "ctx"),
    )
    out_specs = (P("ctx", "head"), P(None, "ctx", None), P(None, "ctx", None))
    return jax.shard_map(local, mesh=mesh, in_specs=in_specs, out_specs=out_specs, check_vma=False)
```

profile of v0, /device:TPU:0, one launch (start us, length us, event | category | flops | bytes accessed | tf_op | source)
XLA Modules:
  0.0 186.1 jit_solution(15703125681996488477)
XLA Ops:
  7.3 1.8 copy.47
  9.2 1.8 copy.48
  12.2 1.1 copy.52
  14.7 23.1 %all-gather = s32[1,2048]{1,0:T(1,128)S(1)} all-gather(s32[1,128]{1,0:T(1,128)S(1)} %constant_dynamic-slice_fusion.3), channel_id=2, replica_groups=mesh['ctx'=16,'head'=2] {'ctx'}, dimensions={1}, use_global_device_ids=true | all-gather | bytes 8704 | tf_op jit(solution)/shard_map/all_gather | solution.py:197
  38.0 20.1 %all_gather.21 = bf16[2048,128]{1,0:T(8,128)(2,1)S(1)} all-gather(bf16[128,128]{1,0:T(8,128)(2,1)S(1)} %fusion.57), channel_id=1, replica_groups=mesh['ctx'=16,'head'=2] {'ctx'}, dimensions={0}, use_global_device_ids=true | all-gather | bytes 557056 | tf_op jit(solution)/shard_map/all_gather | solution.py:195
  58.2 23.6 %all_gather.23 = bf16[2048,128]{1,0:T(8,128)(2,1)} all-gather(bf16[128,128]{1,0:T(8,128)(2,1)S(1)} %fusion.56), channel_id=1, replica_groups=mesh['ctx'=16,'head'=2] {'ctx'}, dimensions={0}, use_global_device_ids=true | all-gather | bytes 557056 | tf_op jit(solution)/shard_map/all_gather | solution.py:196
  81.7 14.5 %while.34 = (s32[]{:T(128)}, f32[128,8,128]{0,2,1:T(8,128)}, bf16[2048,128]{1,0:T(8,128)(2,1)S(1)}, s32[2048]{0:T(1024)S(1)}, bf16[128,8,128]{2,0,1:T(8,128)(2,1...) while((s32[]{:T(128)}, f32[128,8,128]{0,2,1:T(8,128)}, ...), condition=%wide.region_2.3_spmd.clone, body=%wide.region_1.2_spmd.clone.sunk | while | flops 406931456 | bytes 6309588 | solution.py:103
  82.5 2.7 %fusion.93 = f32[128,8,128]{0,2,1:T(8,128)} fusion(f32[512,128,8]{1,0,2:T(8,128)S(1)} %fusion.91, bf16[128,8,128]{2,0,1:T(8,128)(2,1)S(1)} %get-tuple-element.875, f32[8,128]{1,0:T(8,128)S(1)} %bitcast.169, f32[8,128]{1,0:T(8,128)S(1)} %get-tuple-element.873, pred[128,512]{0,1:T(8,128)(4,1)S(1)} %fusion.92, f32[128,8,128]{0,2,1:T(8,128)} %get-tuple-element.855, ...), kind=kOutput, calls=%fused_computation.11.clone.1 | convolution fusion | flops 272367616 | bytes 3745280 | tf_op jit(solution)/shard_map/while/body/eval_jaxpr/gzs,sp->zgp/dot_general | solution.py:99
  86.0 2.9 %fusion.93 = f32[128,8,128]{0,2,1:T(8,128)} fusion(f32[512,128,8]{1,0,2:T(8,128)S(1)} %fusion.91, bf16[128,8,128]{2,0,1:T(8,128)(2,1)S(1)} %get-tuple-element.875, f32[8,128]{1,0:T(8,128)S(1)} %bitcast.169, f32[8,128]{1,0:T(8,128)S(1)} %get-tuple-element.873, pred[128,512]{0,1:T(8,128)(4,1)S(1)} %fusion.92, f32[128,8,128]{0,2,1:T(8,128)} %get-tuple-element.855, ...), kind=kOutput, calls=%fused_computation.11.clone.1 | convolution fusion | flops 272367616 | bytes 3745280 | tf_op jit(solution)/shard_map/while/body/eval_jaxpr/gzs,sp->zgp/dot_general | solution.py:99
  89.7 2.9 %fusion.93 = f32[128,8,128]{0,2,1:T(8,128)} fusion(f32[512,128,8]{1,0,2:T(8,128)S(1)} %fusion.91, bf16[128,8,128]{2,0,1:T(8,128)(2,1)S(1)} %get-tuple-element.875, f32[8,128]{1,0:T(8,128)S(1)} %bitcast.169, f32[8,128]{1,0:T(8,128)S(1)} %get-tuple-element.873, pred[128,512]{0,1:T(8,128)(4,1)S(1)} %fusion.92, f32[128,8,128]{0,2,1:T(8,128)} %get-tuple-element.855, ...), kind=kOutput, calls=%fused_computation.11.clone.1 | convolution fusion | flops 272367616 | bytes 3745280 | tf_op jit(solution)/shard_map/while/body/eval_jaxpr/gzs,sp->zgp/dot_general | solution.py:99
  93.4 2.9 %fusion.93 = f32[128,8,128]{0,2,1:T(8,128)} fusion(f32[512,128,8]{1,0,2:T(8,128)S(1)} %fusion.91, bf16[128,8,128]{2,0,1:T(8,128)(2,1)S(1)} %get-tuple-element.875, f32[8,128]{1,0:T(8,128)S(1)} %bitcast.169, f32[8,128]{1,0:T(8,128)S(1)} %get-tuple-element.873, pred[128,512]{0,1:T(8,128)(4,1)S(1)} %fusion.92, f32[128,8,128]{0,2,1:T(8,128)} %get-tuple-element.855, ...), kind=kOutput, calls=%fused_computation.11.clone.1 | convolution fusion | flops 272367616 | bytes 3745280 | tf_op jit(solution)/shard_map/while/body/eval_jaxpr/gzs,sp->zgp/dot_general | solution.py:99
  98.2 25.1 %all_gather.27 = f32[2048,8]{1,0:T(8,128)S(1)} all-gather(f32[128,8]{1,0:T(8,128)S(1)} %copy.68), channel_id=1, replica_groups=mesh['ctx'=16,'head'=2] {'ctx'}, dimensions={0}, use_global_device_ids=true | all-gather | bytes 69632 | tf_op jit(solution)/shard_map/all_gather | solution.py:218
  123.6 20.4 %all_gather.25 = f32[2048,8]{0,1:T(8,128)S(1)} all-gather(f32[128,8]{0,1:T(8,128)S(1)} %bitcast.170), channel_id=1, replica_groups=mesh['ctx'=16,'head'=2] {'ctx'}, dimensions={0}, use_global_device_ids=true | all-gather | bytes 69632 | tf_op jit(solution)/shard_map/all_gather | solution.py:217
  144.0 29.1 %while.35 = (s32[]{:T(128)}, f32[128,128]{1,0:T(8,128)S(1)}, f32[128,128]{1,0:T(8,128)S(1)}, s32[128]{0:T(128)S(1)}, bf16[2048,1024]{0,1:T(8,128)(2,1)}, /*index...) while((s32[]{:T(128)}, f32[128,128]{1,0:T(8,128)S(1)}, ...), condition=%wide.region_4.5_spmd.clone, body=%wide.region_3.4_spmd.clone.sunk | while | flops 541476480 | bytes 19437560 | solution.py:156
  144.0 1.7 constant_dynamic-slice_fusion.6
  147.8 3.0 %fusion.103 = f32[128,128]{1,0:T(8,128)S(1)} fusion(bf16[512,8,128]{0,2,1:T(8,128)(2,1)} %bitcast.162, f32[8,512,128]{2,1,0:T(8,128)S(1)} %fusion.102, bf16[512,8,128]{0,2,1:T(8,128)(2,1)S(1)} %bitcast.159, f32[8,512]{1,0:T(8,128)S(1)} %get-tuple-element.839, f32[128,128]{1,0:T(8,128)S(1)} %get-tuple-element.898, ...), kind=kOutput, calls=%fused_computation.60.clone.1 | convolution fusion | flops 270565376 | bytes 4374529 | tf_op jit(solution)/shard_map/while/body/eval_jaxpr/lnf,nlb->fb/dot_general | solution.py:148
  151.3 1.7 constant_dynamic-slice_fusion.6
  155.0 3.0 %fusion.103 = f32[128,128]{1,0:T(8,128)S(1)} fusion(bf16[512,8,128]{0,2,1:T(8,128)(2,1)} %bitcast.162, f32[8,512,128]{2,1,0:T(8,128)S(1)} %fusion.102, bf16[512,8,128]{0,2,1:T(8,128)(2,1)S(1)} %bitcast.159, f32[8,512]{1,0:T(8,128)S(1)} %get-tuple-element.839, f32[128,128]{1,0:T(8,128)S(1)} %get-tuple-element.898, ...), kind=kOutput, calls=%fused_computation.60.clone.1 | convolution fusion | flops 270565376 | bytes 4374529 | tf_op jit(solution)/shard_map/while/body/eval_jaxpr/lnf,nlb->fb/dot_general | solution.py:148
  158.5 1.7 constant_dynamic-slice_fusion.6
  162.3 3.0 %fusion.103 = f32[128,128]{1,0:T(8,128)S(1)} fusion(bf16[512,8,128]{0,2,1:T(8,128)(2,1)} %bitcast.162, f32[8,512,128]{2,1,0:T(8,128)S(1)} %fusion.102, bf16[512,8,128]{0,2,1:T(8,128)(2,1)S(1)} %bitcast.159, f32[8,512]{1,0:T(8,128)S(1)} %get-tuple-element.839, f32[128,128]{1,0:T(8,128)S(1)} %get-tuple-element.898, ...), kind=kOutput, calls=%fused_computation.60.clone.1 | convolution fusion | flops 270565376 | bytes 4374529 | tf_op jit(solution)/shard_map/while/body/eval_jaxpr/lnf,nlb->fb/dot_general | solution.py:148
  165.8 1.7 constant_dynamic-slice_fusion.6
  169.6 3.0 %fusion.103 = f32[128,128]{1,0:T(8,128)S(1)} fusion(bf16[512,8,128]{0,2,1:T(8,128)(2,1)} %bitcast.162, f32[8,512,128]{2,1,0:T(8,128)S(1)} %fusion.102, bf16[512,8,128]{0,2,1:T(8,128)(2,1)S(1)} %bitcast.159, f32[8,512]{1,0:T(8,128)S(1)} %get-tuple-element.839, f32[128,128]{1,0:T(8,128)S(1)} %get-tuple-element.898, ...), kind=kOutput, calls=%fused_computation.60.clone.1 | convolution fusion | flops 270565376 | bytes 4374529 | tf_op jit(solution)/shard_map/while/body/eval_jaxpr/lnf,nlb->fb/dot_general | solution.py:148
  173.1 1.5 collective-permute-start
  175.3 1.8 collective-permute-done
  (100 shorter events, 20.9 us)
Async XLA Ops:
  7.2 7.5 %copy-start = (s32[2,128]{1,0:T(2,128)S(1)}, s32[2,128]{1,0:T(2,128)}, u32[]{:S(2)}) copy-start(s32[2,128]{1,0:T(2,128)} %param.18) | copy-start | bytes 3076
  7.2 6.2 %copy-start.2 = (bf16[128,1024]{1,0:T(8,128)(2,1)S(1)}, bf16[128,1024]{1,0:T(8,128)(2,1)}, u32[]{:S(2)}) copy-start(bf16[128,1024]{1,0:T(8,128)(2,1)} %param.19) | copy-start | bytes 786436
  7.2 30.6 %copy-start.6 = (f32[2,128]{1,0:T(2,128)S(1)}, f32[2,128]{1,0:T(2,128)}, u32[]{:S(2)}) copy-start(f32[2,128]{1,0:T(2,128)} %param.15) | copy-start | bytes 3076
  7.2 30.6 %copy-start.7 = (f32[2,128]{1,0:T(2,128)S(1)}, f32[2,128]{1,0:T(2,128)}, u32[]{:S(2)}) copy-start(f32[2,128]{1,0:T(2,128)} %param.17) | copy-start | bytes 3076
  7.2 30.6 %copy-start.3 = (bf16[2,128,128]{2,1,0:T(8,128)(2,1)S(1)}, bf16[2,128,128]{2,1,0:T(8,128)(2,1)}, u32[]{:S(2)}) copy-start(bf16[2,128,128]{2,1,0:T(8,128)(2,1)} %param.14) | copy-start | bytes 196612
  7.2 30.7 %copy-start.4 = (bf16[2,128,128]{2,1,0:T(8,128)(2,1)S(1)}, bf16[2,128,128]{2,1,0:T(8,128)(2,1)}, u32[]{:S(2)}) copy-start(bf16[2,128,128]{2,1,0:T(8,128)(2,1)} %param.16) | copy-start | bytes 196612
  7.2 136.7 %all-gather.4.cloned.1.call-start = ((), (), s32[]{:S(2)}) async-start(), calls=%async_computation | async-start | bytes 4456448 | tf_op jit(solution)/shard_map/all_gather | solution.py:211
  9.1 72.6 %copy-start.5 = (f32[8,128]{1,0:T(8,128)S(1)}, f32[8,128]{1,0:T(8,128)}, u32[]{:S(2)}) copy-start(f32[8,128]{1,0:T(8,128)} %param.21) | copy-start | bytes 12292
  9.1 134.8 %all-gather.6.cloned.1.call-start = ((), (), s32[]{:S(2)}) async-start(), calls=%async_computation.1 | async-start | bytes 4456448 | tf_op jit(solution)/shard_map/all_gather | solution.py:214
  145.7 1.1 copy-start.1
  153.0 1.1 copy-start.1
  160.2 1.1 copy-start.1
  167.5 1.1 copy-start.1
  173.1 4.0 %collective-permute-start = (bf16[128,128]{1,0:T(8,128)(2,1)S(1)}, bf16[128,128]{1,0:T(8,128)(2,1)S(1)}, u32[]{:S(2)}, u32[]{:S(2)}) collective-permute-start(bf16[128,128]{1,0:T(8,128)(2,1)S(1)} %convert_element_type.96), channel_id=1, source_target_pairs={{0,1},{1,0},{2,3},{3,2},{4,5},{5,4},{6,7},{7,6},{8,9},{9,8},{10,11... | collective-permute-start | bytes 98312 | tf_op jit(solution)/shard_map/ppermute | solution.py:20
  174.6 4.0 %collective-permute-start.1 = (bf16[128,128]{1,0:T(8,128)(2,1)S(1)}, bf16[128,128]{1,0:T(8,128)(2,1)S(1)}, u32[]{:S(2)}, u32[]{:S(2)}) collective-permute-start(bf16[128,128]{1,0:T(8,128)(2,1)S(1)} %convert_element_type.97), channel_id=1, source_target_pairs={{0,1},{1,0},{2,3},{3,2},{4,5},{5,4},{6,7},{7,6},{8,9},{9,8},{10,11... | collective-permute-start | bytes 98312 | tf_op jit(solution)/shard_map/ppermute | solution.py:20
Sparse Core Ops, SparseCore 0:
  10.2 58.7 all-gather.3
  71.2 60.0 all-gather.5
where the time goes:
time: 187 us; the launch traced here: 186 us
  blocking collectives  112 us (60%)
  matrix products  31.1 us (17%)
  local copies, waits for them, and re-layouts  17.5 us (9%)
  between operations  14.3 us (8%)
  other arithmetic  5.63 us (3%)
  waiting for transfers between devices  2.77 us (1%)
  starting transfers between devices  2.24 us (1%)
    all_gather x1, blocking collectives, local(): delta_piece = lax.all_gather(row_delta, 'ctx', axis=0, tiled=True)  25.1 us
    all_gather x1, blocking collectives, local(): value_piece = lax.all_gather(value_rows, 'ctx', axis=0, tiled=True)  23.6 us
    all_gather x1, blocking collectives, local(): evict_piece = lax.all_gather(evicted, 'ctx', axis=0, tiled=True)  23.1 us
    all_gather x1, blocking collectives, local(): norm_piece = lax.all_gather(norm_rows, 'ctx', axis=0, tiled=True)  20.4 us
    all_gather x1, blocking collectives, local(): key_piece = lax.all_gather(key_rows, 'ctx', axis=0, tiled=True)  20.1 us
    dot_general x4, matrix products, key_sub_block(): jnp.einsum('lnf,nlb->fb', score_gradient, query_block_rows, preferred_ele...  11.9 us
    dot_general x4, matrix products, query_sub_block(): jnp.einsum('gzs,sp->zgp', score_gradient, key_block_rows, preferred_eleme...  11.4 us
    dynamic_slice x4, local copies, waits for them, and re-layouts, key_sub_block(): lax.dynamic_slice_in_dim(grad_piece, within, step_len, 0)  6.76 us
  transfers between devices with their start and end apart: 4, of which 2 were waited for; matrix products, arithmetic and copies ran while one was open for 12% of the time, Pallas kernels for 0%

commit v1 on v0

v1 whole, which is shorter than its diff:
```python
import functools
import math

import jax
import jax.numpy as jnp
from jax import lax
from jax.experimental import pallas as pl
from jax.experimental.pallas import tpu as pltpu
from jax.sharding import PartitionSpec as P

ASKER_PROJ_NUM = 16
KEY_VALUE_HEADS = 2
DELAY = 256
FLAG_ROWS = 16
LOG2E = math.log2(math.e)
MESH = pl.DeviceIdType.MESH


def kernel(
    n,
    head_devices,
    q_ref,
    kc_ref,
    ks_ref,
    vc_ref,
    vs_ref,
    ev_ref,
    of_ref,
    go_ref,
    ln_ref,
    dq_ref,
    dk_ref,
    dv_ref,
    kv,
    part,
    core_in,
    y_in,
    z_in,
    q_rows,
    g_rows,
    q_cols,
    g_cols,
    norm,
    delta,
    dq_acc,
    group_sum,
    head_out,
    head_in,
    kz_send,
    kz_recv,
    ky_send,
    ky_recv,
    kc_send,
    kc_recv,
    rc_send,
    rc_recv,
    ry_send,
    ry_recv,
    rz_send,
    rz_recv,
    gs_send,
    gs_recv,
    h_send,
    h_recv,
):
    tokens, _ = q_ref.shape
    width = kc_ref.shape[2]
    heads = ln_ref.shape[0]
    half = tokens // 2
    zs = n // 4
    low_rows = 2 * half + FLAG_ROWS
    all_rows = 4 * half + FLAG_ROWS
    per_group = head_devices // KEY_VALUE_HEADS
    scale = width ** (-0.5)

    me = lax.axis_index("ctx")
    hd = lax.axis_index("head")
    c = lax.rem(me, 2)
    y = lax.rem(me // 2, 2)
    z = me // 4
    group = hd // per_group
    member = lax.rem(hd, per_group)

    def at(zi, yi, ci):
        return (zi * 4 + yi * 2 + ci, hd)

    core_peer = at(z, y, 1 - c)
    y_peer = at(z, 1 - y, c)
    other_group = (me, lax.rem(hd + per_group, head_devices))

    def turn(s):
        if zs & (zs - 1):
            return lax.rem(z + s, zs)
        out = 0
        bit = 1
        while bit < zs:
            out = out + lax.rem(z // bit + s // bit, 2) * bit
            bit *= 2
        return out

    barrier = pltpu.get_barrier_semaphore()
    pl.semaphore_signal(barrier, inc=1, device_id=core_peer, device_id_type=MESH)
    pl.semaphore_signal(barrier, inc=1, device_id=y_peer, device_id_type=MESH)
    pl.semaphore_signal(barrier, inc=1, device_id=other_group, device_id_type=MESH)
    for s in range(1, zs):
        pl.semaphore_signal(
            barrier, inc=1, device_id=at(turn(s), y, c), device_id_type=MESH
        )
    for s in range(1, per_group):
        pl.semaphore_signal(
            barrier,
            inc=1,
            device_id=(me, group * per_group + lax.rem(member + s, per_group)),
            device_id_type=MESH,
        )

    def column(row):
        return jnp.transpose(jnp.broadcast_to(row, (tokens, tokens)))

    key_col = column(ks_ref[pl.ds(group, 1), :])
    value_col = column(vs_ref[pl.ds(group, 1), :])
    keys = (kc_ref[group].astype(jnp.float32) * key_col).astype(jnp.bfloat16)
    values = (vc_ref[group].astype(jnp.float32) * value_col).astype(jnp.bfloat16)
    flags = ev_ref[pl.ds(group, 1), :].astype(jnp.float32)
    own = kv.at[z, y, c]
    own[0:half, :] = keys[0:half]
    own[half : 2 * half, :] = values[0:half]
    own[2 * half : low_rows, :] = jnp.broadcast_to(flags, (FLAG_ROWS, tokens)).astype(
        jnp.bfloat16
    )
    own[low_rows : low_rows + half, :] = keys[half:]
    own[low_rows + half :, :] = values[half:]

    pl.semaphore_wait(barrier, 3 + (zs - 1) + (per_group - 1))

    def sized(whole, f, full, low):
        @pl.when(whole)
        def _():
            f(pl.ds(0, full))

        @pl.when(jnp.logical_not(whole))
        def _():
            f(pl.ds(0, low))

    def kz_copy(src_z, dst_z, rows):
        return pltpu.make_async_remote_copy(
            src_ref=kv.at[z, y, c, rows],
            dst_ref=kv.at[src_z, y, c, rows],
            send_sem=kz_send.at[dst_z],
            recv_sem=kz_recv.at[src_z],
            device_id=at(dst_z, y, c),
            device_id_type=MESH,
        )

    def ky_copy(zi, yi, rows):
        ref = kv.at[zi, yi, c, rows]
        return pltpu.make_async_remote_copy(
            src_ref=ref,
            dst_ref=ref,
            send_sem=ky_send.at[zi],
            recv_sem=ky_recv.at[zi],
            device_id=y_peer,
            device_id_type=MESH,
        )

    def kc_copy(zi, ci, rows):
        ref = kv.at[zi, :, ci, rows]
        return pltpu.make_async_remote_copy(
            src_ref=ref,
            dst_ref=ref,
            send_sem=kc_send.at[zi],
            recv_sem=kc_recv.at[zi],
            device_id=core_peer,
            device_id_type=MESH,
        )

    def send_z(s, carry):
        zi = turn(s)
        sized(z >= zi, lambda rows: kz_copy(z, zi, rows).start(), all_rows, low_rows)
        return carry

    lax.fori_loop(1, zs, send_z, 0)

    def forward_y(s):
        zi = turn(s)

        def go(rows):
            @pl.when(zi != z)
            def _():
                kz_copy(zi, zi, rows).wait_recv()

            ky_copy(zi, y, rows).start()

        sized(zi >= z, go, all_rows, low_rows)

    def forward_c(s):
        zi = turn(s)

        def go(rows):
            ky_copy(zi, 1 - y, rows).wait_recv()
            kc_copy(zi, c, rows).start()

        sized(zi >= z, go, all_rows, low_rows)

    def ready(s):
        zi = turn(s)
        sized(
            zi >= z,
            lambda rows: kc_copy(zi, 1 - c, rows).wait_recv(),
            all_rows,
            low_rows,
        )

    forward_y(0)

    for side in range(2):
        tok = slice(side * half, (side + 1) * half)

        def by_head(ref):
            return jnp.concatenate(
                [ref[tok, h * width : (h + 1) * width] for h in range(heads)], axis=0
            )

        q = by_head(q_ref)
        g = by_head(go_ref)
        q_rows[side] = q
        g_rows[side] = g
        q_cols[side] = jnp.transpose(q)
        g_t = jnp.transpose(g)
        g_cols[side] = g_t
        o_t = jnp.transpose(by_head(of_ref))
        delta[side] = jnp.sum(
            g_t.astype(jnp.float32) * o_t.astype(jnp.float32), axis=0, keepdims=True
        )
        norm[side] = (
            jnp.concatenate([ln_ref[h : h + 1, tok] for h in range(heads)], axis=1)
            * LOG2E
        )
        dq_acc[side] = jnp.zeros(dq_acc.shape[1:], jnp.float32)

    chunk = 4 * half
    lanes = 2 * half
    copies = heads * half // lanes
    row = lax.broadcasted_iota(jnp.int32, (chunk, lanes), 0)
    lane = lax.broadcasted_iota(jnp.int32, (chunk, lanes), 1)
    row_block = row // half
    row_in = lax.rem(row, half)
    lane_in = lax.rem(lane, half)

    def terms(k, v, k_t, key_pos, limit, side):
        block = me if side == 0 else 2 * n - 1 - me
        distance = block * half + lane_in - key_pos
        visible = (distance >= 0) & (distance < limit)
        bias = jnp.where(visible, 0.0, -1e30)
        bias = jnp.concatenate([bias] * copies, axis=1)
        scores = jnp.dot(k, q_cols[side], preferred_element_type=jnp.float32)
        weights = jnp.exp2(scores * (scale * LOG2E) - norm[side] + bias)
        dweights = jnp.dot(v, g_cols[side], preferred_element_type=jnp.float32)
        dscores = (scale * weights * (dweights - delta[side])).astype(jnp.bfloat16)
        weights = weights.astype(jnp.bfloat16)
        dq_acc[side] += jnp.dot(k_t, dscores, preferred_element_type=jnp.float32)
        dk = jnp.dot(dscores, q_rows[side], preferred_element_type=jnp.float32)
        dv = jnp.dot(weights, g_rows[side], preferred_element_type=jnp.float32)
        return dk.reshape(2, 2, half, width), dv.reshape(2, 2, half, width)

    def limits(zi, first):
        cols = [
            column(kv[zi, yi, ci, 2 * half : 2 * half + FLAG_ROWS, :].astype(jnp.float32)[0:1])[
                first : first + half
            ]
            for yi in range(2)
            for ci in range(2)
        ]
        evicted = jnp.concatenate(cols, axis=0)
        return jnp.where(evicted == 0.0, 2 * n * half, DELAY)

    def compute(s):
        zi = turn(s)
        k = kv[zi, :, :, 0:half, :].reshape(chunk, width)
        v = kv[zi, :, :, half : 2 * half, :].reshape(chunk, width)
        k_t = jnp.transpose(k)
        key_pos = (zi * 4 + row_block) * half + row_in
        limit = limits(zi, 0)
        dk, dv = terms(k, v, k_t, key_pos, limit, 1)
        part[zi, :, :, 0:half, :] = dk
        part[zi, :, :, half : 2 * half, :] = dv

        @pl.when(zi <= z)
        def _():
            dk, dv = terms(k, v, k_t, key_pos, limit, 0)
            part[zi, :, :, 0:half, :] += dk
            part[zi, :, :, half : 2 * half, :] += dv

        @pl.when(zi >= z)
        def _():
            k = kv[zi, :, :, low_rows : low_rows + half, :].reshape(chunk, width)
            v = kv[zi, :, :, low_rows + half :, :].reshape(chunk, width)
            key_pos = (2 * n - 1 - zi * 4 - row_block) * half + row_in
            dk, dv = terms(k, v, jnp.transpose(k), key_pos, limits(zi, half), 1)
            part[zi, :, :, 2 * half : 3 * half, :] = dk
            part[zi, :, :, 3 * half :, :] = dv

    def rc_copy(zi, rows):
        return pltpu.make_async_remote_copy(
            src_ref=part.at[zi, :, 1 - c, rows],
            dst_ref=core_in.at[zi, :, rows],
            send_sem=rc_send.at[zi],
            recv_sem=rc_recv.at[zi],
            device_id=core_peer,
            device_id_type=MESH,
        )

    def ry_copy(zi, rows):
        return pltpu.make_async_remote_copy(
            src_ref=part.at[zi, 1 - y, c, rows],
            dst_ref=y_in.at[zi, rows],
            send_sem=ry_send.at[zi],
            recv_sem=ry_recv.at[zi],
            device_id=y_peer,
            device_id_type=MESH,
        )

    def rz_copy(src_z, dst_z, rows):
        return pltpu.make_async_remote_copy(
            src_ref=part.at[dst_z, y, c, rows],
            dst_ref=z_in.at[src_z, rows],
            send_sem=rz_send.at[dst_z],
            recv_sem=rz_recv.at[src_z],
            device_id=at(dst_z, y, c),
            device_id_type=MESH,
        )

    def reduce_c(s):
        zi = turn(s)
        sized(zi >= z, lambda rows: rc_copy(zi, rows).start(), 4 * half, 2 * half)

    def reduce_y(s):
        zi = turn(s)

        def go(rows):
            rc_copy(zi, rows).wait_recv()
            for yi in range(2):
                part[zi, yi, c, rows, :] += core_in[zi, yi, rows, :]
            ry_copy(zi, rows).start()

        sized(zi >= z, go, 4 * half, 2 * half)

    def reduce_z(s):
        zi = turn(s)

        def go(rows):
            ry_copy(zi, rows).wait_recv()
            part[zi, y, c, rows, :] += y_in[zi, rows, :]

            @pl.when(zi != z)
            def _():
                rz_copy(z, zi, rows).start()

        sized(zi >= z, go, 4 * half, 2 * half)

    def when(cond, f, s):
        @pl.when(cond)
        def _():
            f(s)

    forward_y(1)
    forward_c(0)

    def step(s, carry):
        when(s + 2 < zs, forward_y, s + 2)
        when(s + 1 < zs, forward_c, s + 1)
        ready(s)
        compute(s)
        reduce_c(s)
        when(s >= 1, reduce_y, s - 1)
        when(s >= 2, reduce_z, s - 2)
        return carry

    lax.fori_loop(0, zs, step, 0)
    reduce_y(zs - 1)
    if zs >= 2:
        reduce_z(zs - 2)
    reduce_z(zs - 1)

    for side in range(2):
        dq = jnp.transpose(dq_acc[side]).astype(jnp.bfloat16)
        for h in range(heads):
            dq_ref[side * half : (side + 1) * half, h * width : (h + 1) * width] = dq[
                h * half : (h + 1) * half
            ]

    def collect(s, carry):
        zi = turn(s)

        def go(rows):
            rz_copy(zi, zi, rows).wait_recv()
            part[z, y, c, rows, :] += z_in[zi, rows, :]

        sized(z >= zi, go, 4 * half, 2 * half)
        return carry

    lax.fori_loop(1, zs, collect, 0)

    total = part[z, y, c]
    if per_group > 1:
        group_sum[member] = total

        def gs_copy(src, s):
            return pltpu.make_async_remote_copy(
                src_ref=group_sum.at[member],
                dst_ref=group_sum.at[src],
                send_sem=gs_send.at[s],
                recv_sem=gs_recv.at[src],
                device_id=(me, group * per_group + lax.rem(member + s, per_group)),
                device_id_type=MESH,
            )

        for s in range(1, per_group):
            gs_copy(member, s).start()
        for s in range(1, per_group):
            gs_copy(lax.rem(member + s, per_group), s).wait_recv()
        for s in range(1, per_group):
            gs_copy(member, s).wait_send()
        total = group_sum[0]
        for s in range(1, per_group):
            total = total + group_sum[s]

    head_out[...] = total.astype(jnp.bfloat16)
    h_copy = pltpu.make_async_remote_copy(
        src_ref=head_out,
        dst_ref=head_in,
        send_sem=h_send,
        recv_sem=h_recv,
        device_id=other_group,
        device_id_type=MESH,
    )
    h_copy.start()

    def put(index, block):
        dk_ref[index, 0:half, :] = block[0:half, :]
        dv_ref[index, 0:half, :] = block[half : 2 * half, :]
        dk_ref[index, half:, :] = block[2 * half : 3 * half, :]
        dv_ref[index, half:, :] = block[3 * half :, :]

    put(group, head_out)

    def sent(s, carry):
        zi = turn(s)

        def own_z(rows):
            kz_copy(z, zi, rows).wait_send()

        def kept(rows):
            ky_copy(zi, y, rows).wait_send()
            kc_copy(zi, c, rows).wait_send()

        def summed(rows):
            rc_copy(zi, rows).wait_send()
            ry_copy(zi, rows).wait_send()

            @pl.when(zi != z)
            def _():
                rz_copy(z, zi, rows).wait_send()

        @pl.when(zi != z)
        def _():
            sized(z >= zi, own_z, all_rows, low_rows)

        sized(zi >= z, kept, all_rows, low_rows)
        sized(zi >= z, summed, 4 * half, 2 * half)
        return carry

    lax.fori_loop(0, zs, sent, 0)
    h_copy.wait()
    put(1 - group, head_in)


def local(
    queries,
    key_codes,
    key_scale,
    value_codes,
    value_scale,
    evict_flags,
    out_forward,
    grad_output,
    log_norm,
):
    n = lax.axis_size("ctx")
    head_devices = lax.axis_size("head")
    per_group = head_devices // KEY_VALUE_HEADS
    tokens = queries.shape[0]
    heads = log_norm.shape[0]
    width = key_codes.shape[2]
    half = tokens // 2
    zs = n // 4
    side_rows = heads * half
    f32, bf16 = jnp.float32, jnp.bfloat16
    vmem = pl.BlockSpec(memory_space=pltpu.VMEM)
    dma = pltpu.SemaphoreType.DMA
    return pl.pallas_call(
        functools.partial(kernel, n, head_devices),
        out_shape=(
            jax.ShapeDtypeStruct(queries.shape, bf16),
            jax.ShapeDtypeStruct(key_codes.shape, bf16),
            jax.ShapeDtypeStruct(value_codes.shape, bf16),
        ),
        in_specs=[vmem] * 9,
        out_specs=(vmem, vmem, vmem),
        scratch_shapes=[
            pltpu.VMEM((zs, 2, 2, 4 * half + FLAG_ROWS, width), bf16),
            pltpu.VMEM((zs, 2, 2, 4 * half, width), f32),
            pltpu.VMEM((zs, 2, 4 * half, width), f32),
            pltpu.VMEM((zs, 4 * half, width), f32),
            pltpu.VMEM((zs, 4 * half, width), f32),
            pltpu.VMEM((2, side_rows, width), bf16),
            pltpu.VMEM((2, side_rows, width), bf16),
            pltpu.VMEM((2, width, side_rows), bf16),
            pltpu.VMEM((2, width, side_rows), bf16),
            pltpu.VMEM((2, 1, side_rows), f32),
            pltpu.VMEM((2, 1, side_rows), f32),
            pltpu.VMEM((2, width, side_rows), f32),
            pltpu.VMEM((per_group, 4 * half, width), f32),
            pltpu.VMEM((4 * half, width), bf16),
            pltpu.VMEM((4 * half, width), bf16),
        ]
        + [dma((zs,))] * 12
        + [dma((per_group,))] * 2
        + [dma] * 2,
        compiler_params=pltpu.CompilerParams(
            collective_id=0, has_side_effects=True, vmem_limit_bytes=48 * 2**20
        ),
    )(
        queries,
        key_codes,
        key_scale,
        value_codes,
        value_scale,
        evict_flags,
        out_forward,
        grad_output,
        log_norm,
    )


def solution(mesh):
    in_specs = (
        P("ctx", "head"),
        P(None, "ctx", None),
        P(None, "ctx"),
        P(None, "ctx", None),
        P(None, "ctx"),
        P(None, "ctx"),
        P("ctx", "head"),
        P("ctx", "head"),
        P("head", "ctx"),
    )
    out_specs = (P("ctx", "head"), P(None, "ctx", None), P(None, "ctx", None))
    return jax.shard_map(local, mesh=mesh, in_specs=in_specs, out_specs=out_specs, check_vma=False)
```

time: 187 us -> 49.6 us (0.27)
  the two profiles are of different devices: /device:TPU:0 before, /device:TPU:16 now
where the time goes in v1:
time: 49.6 us; the launch traced here: 49.2 us
  Pallas kernels  39.4 us (79%)
  local copies, waits for them, and re-layouts  9.2 us (19%)
  between operations  0.66 us (1%)
    pallas_call x1, Pallas kernels, local(): pl.pallas_call(functools.partial(kernel, n, head_devices), out_shape=(jax...  39.4 us
    unnamed x21, local copies, waits for them, and re-layouts  9.2 us

profile of v1, /device:TPU:16, one launch (start us, length us, event | category | flops | bytes accessed | tf_op | source)
XLA Modules:
  0.0 49.2 jit_solution(16020886215937566133)
XLA Ops:
  0.6 0.0 copy-start
  0.6 0.9 %copy-done = bf16[128,1024]{1,0:T(8,128)(2,1)S(1)} copy-done((bf16[128,1024]{1,0:T(8,128)(2,1)S(1)}, bf16[128,1024]{1,0:T(8,128)(2,1)}, u32[]{:S(2)}) %copy-start) | copy-done | bytes 262168
  1.6 0.0 copy-start.1
  1.6 0.9 %copy-done.1 = bf16[128,1024]{1,0:T(8,128)(2,1)S(1)} copy-done((bf16[128,1024]{1,0:T(8,128)(2,1)S(1)}, bf16[128,1024]{1,0:T(8,128)(2,1)}, u32[]{:S(2)}) %copy-start.1) | copy-done | bytes 262168
  2.5 0.0 copy-start.2
  2.5 0.9 %copy-done.2 = bf16[128,1024]{1,0:T(8,128)(2,1)S(1)} copy-done((bf16[128,1024]{1,0:T(8,128)(2,1)S(1)}, bf16[128,1024]{1,0:T(8,128)(2,1)}, u32[]{:S(2)}) %copy-start.2) | copy-done | bytes 262168
  3.5 0.0 copy-start.3
  3.5 0.8 %copy-done.3 = bf16[2,128,128]{2,1,0:T(8,128)(2,1)S(1)} copy-done((bf16[2,128,128]{2,1,0:T(8,128)(2,1)S(1)}, bf16[2,128,128]{2,1,0:T(8,128)(2,1)}, u32[]{:S(2)}) %copy-start.3) | copy-done | bytes 65560
  4.3 0.0 copy-start.4
  4.3 0.8 %copy-done.4 = bf16[2,128,128]{2,1,0:T(8,128)(2,1)S(1)} copy-done((bf16[2,128,128]{2,1,0:T(8,128)(2,1)S(1)}, bf16[2,128,128]{2,1,0:T(8,128)(2,1)}, u32[]{:S(2)}) %copy-start.4) | copy-done | bytes 65560
  5.2 0.0 copy-start.5
  5.2 0.7 %copy-done.5 = f32[8,128]{1,0:T(8,128)S(1)} copy-done((f32[8,128]{1,0:T(8,128)S(1)}, f32[8,128]{1,0:T(8,128)}, u32[]{:S(2)}) %copy-start.5) | copy-done | bytes 4120
  5.9 0.0 copy-start.6
  5.9 0.7 %copy-done.6 = f32[2,128]{1,0:T(2,128)S(1)} copy-done((f32[2,128]{1,0:T(2,128)S(1)}, f32[2,128]{1,0:T(2,128)}, u32[]{:S(2)}) %copy-start.6) | copy-done | bytes 1048
  6.5 0.0 copy-start.7
  6.5 0.7 %copy-done.7 = f32[2,128]{1,0:T(2,128)S(1)} copy-done((f32[2,128]{1,0:T(2,128)S(1)}, f32[2,128]{1,0:T(2,128)}, u32[]{:S(2)}) %copy-start.7) | copy-done | bytes 1048
  7.2 0.0 copy-start.8
  7.2 0.7 %copy-done.8 = s32[2,128]{1,0:T(2,128)S(1)} copy-done((s32[2,128]{1,0:T(2,128)S(1)}, s32[2,128]{1,0:T(2,128)}, u32[]{:S(2)}) %copy-start.8) | copy-done | bytes 1048
  7.9 39.4 %shard_map.112 = (bf16[128,1024]{1,0:T(8,128)(2,1)S(1)}, bf16[2,128,128]{2,1,0:T(8,128)(2,1)S(1)}, bf16[2,128,128]{2,1,0:T(8,128)(2,1)S(1)}) custom-call(bf16[128,1024]{1,0:T(8,128)(2,1)S(1)} %copy-done, bf16[2,128,128]{2,1,0:T(8,128)(2,1)S(1)} %copy-done.3, f32[2,128]{1,0:T(2,128)S(1)} %copy-done.6, bf16[2,128,128]{2,1,0:T(8,128)(2,1)S(1)} %copy-done.4, ...), custom_call_target="tpu_custom_call" | custom-call | tf_op jit(solution)/shard_map/pallas_call | solution.py:501
  47.3 0.7 %copy.15 = bf16[128,1024]{1,0:T(8,128)(2,1)} copy(bf16[128,1024]{1,0:T(8,128)(2,1)S(1)} %get-tuple-element.6) | data formatting | bytes 524288
  48.0 0.6 %copy.16 = bf16[2,128,128]{2,1,0:T(8,128)(2,1)} copy(bf16[2,128,128]{2,1,0:T(8,128)(2,1)S(1)} %get-tuple-element.7) | data formatting | bytes 131072
  48.6 0.6 %copy.17 = bf16[2,128,128]{2,1,0:T(8,128)(2,1)} copy(bf16[2,128,128]{2,1,0:T(8,128)(2,1)S(1)} %get-tuple-element.8) | data formatting | bytes 131072
Async XLA Ops:
  0.6 1.0 %copy-start = (bf16[128,1024]{1,0:T(8,128)(2,1)S(1)}, bf16[128,1024]{1,0:T(8,128)(2,1)}, u32[]{:S(2)}) copy-start(bf16[128,1024]{1,0:T(8,128)(2,1)} %q_ref.1) | copy-start | bytes 786436
  1.6 0.9 %copy-start.1 = (bf16[128,1024]{1,0:T(8,128)(2,1)S(1)}, bf16[128,1024]{1,0:T(8,128)(2,1)}, u32[]{:S(2)}) copy-start(bf16[128,1024]{1,0:T(8,128)(2,1)} %of_ref.1) | copy-start | bytes 786436
  2.5 0.9 %copy-start.2 = (bf16[128,1024]{1,0:T(8,128)(2,1)S(1)}, bf16[128,1024]{1,0:T(8,128)(2,1)}, u32[]{:S(2)}) copy-start(bf16[128,1024]{1,0:T(8,128)(2,1)} %go_ref.1) | copy-start | bytes 786436
  3.5 0.8 %copy-start.3 = (bf16[2,128,128]{2,1,0:T(8,128)(2,1)S(1)}, bf16[2,128,128]{2,1,0:T(8,128)(2,1)}, u32[]{:S(2)}) copy-start(bf16[2,128,128]{2,1,0:T(8,128)(2,1)} %kc_ref.1) | copy-start | bytes 196612
  4.3 0.8 %copy-start.4 = (bf16[2,128,128]{2,1,0:T(8,128)(2,1)S(1)}, bf16[2,128,128]{2,1,0:T(8,128)(2,1)}, u32[]{:S(2)}) copy-start(bf16[2,128,128]{2,1,0:T(8,128)(2,1)} %vc_ref.1) | copy-start | bytes 196612
  5.2 0.7 %copy-start.5 = (f32[8,128]{1,0:T(8,128)S(1)}, f32[8,128]{1,0:T(8,128)}, u32[]{:S(2)}) copy-start(f32[8,128]{1,0:T(8,128)} %ln_ref.1) | copy-start | bytes 12292
  5.9 0.7 %copy-start.6 = (f32[2,128]{1,0:T(2,128)S(1)}, f32[2,128]{1,0:T(2,128)}, u32[]{:S(2)}) copy-start(f32[2,128]{1,0:T(2,128)} %ks_ref.1) | copy-start | bytes 3076
  6.5 0.7 %copy-start.7 = (f32[2,128]{1,0:T(2,128)S(1)}, f32[2,128]{1,0:T(2,128)}, u32[]{:S(2)}) copy-start(f32[2,128]{1,0:T(2,128)} %vs_ref.1) | copy-start | bytes 3076
  7.2 0.7 %copy-start.8 = (s32[2,128]{1,0:T(2,128)S(1)}, s32[2,128]{1,0:T(2,128)}, u32[]{:S(2)}) copy-start(s32[2,128]{1,0:T(2,128)} %ev_ref.1) | copy-start | bytes 3076

commit v2 on v1

--- a/solution.py
+++ b/solution.py
@@ -19,15 +19,15 @@
 def kernel(
     n,
     head_devices,
-    q_ref,
-    kc_ref,
-    ks_ref,
-    vc_ref,
-    vs_ref,
-    ev_ref,
-    of_ref,
-    go_ref,
-    ln_ref,
+    q_hbm,
+    kc_hbm,
+    ks_hbm,
+    vc_hbm,
+    vs_hbm,
+    ev_hbm,
+    of_hbm,
+    go_hbm,
+    ln_hbm,
     dq_ref,
     dk_ref,
     dv_ref,
@@ -36,6 +36,8 @@
     core_in,
     y_in,
     z_in,
+    y_out,
+    z_out,
     q_rows,
     g_rows,
     q_cols,
@@ -62,9 +64,19 @@
     gs_recv,
     h_send,
     h_recv,
+    q_ref,
+    kc_ref,
+    ks_ref,
+    vc_ref,
+    vs_ref,
+    ev_ref,
+    of_ref,
+    go_ref,
+    ln_ref,
+    in_sems,
 ):
     tokens, _ = q_ref.shape
-    width = kc_ref.shape[2]
+    width = kc_ref.shape[1]
     heads = ln_ref.shape[0]
     half = tokens // 2
     zs = n // 4
@@ -114,13 +126,36 @@
             device_id_type=MESH,
         )
 
+    kv_loads = [
+        pltpu.make_async_copy(src, dst, in_sems.at[i])
+        for i, (src, dst) in enumerate(
+            [
+                (ks_hbm, ks_ref),
+                (kc_hbm.at[group], kc_ref),
+                (vs_hbm, vs_ref),
+                (vc_hbm.at[group], vc_ref),
+                (ev_hbm, ev_ref),
+            ]
+        )
+    ]
+    query_loads = [
+        pltpu.make_async_copy(src, dst, in_sems.at[len(kv_loads) + i])
+        for i, (src, dst) in enumerate(
+            [(q_hbm, q_ref), (go_hbm, go_ref), (of_hbm, of_ref), (ln_hbm, ln_ref)]
+        )
+    ]
+    for load in kv_loads + query_loads:
+        load.start()
+    for load in kv_loads:
+        load.wait()
+
     def column(row):
         return jnp.transpose(jnp.broadcast_to(row, (tokens, tokens)))
 
     key_col = column(ks_ref[pl.ds(group, 1), :])
     value_col = column(vs_ref[pl.ds(group, 1), :])
-    keys = (kc_ref[group].astype(jnp.float32) * key_col).astype(jnp.bfloat16)
-    values = (vc_ref[group].astype(jnp.float32) * value_col).astype(jnp.bfloat16)
+    keys = (kc_ref[...].astype(jnp.float32) * key_col).astype(jnp.bfloat16)
+    values = (vc_ref[...].astype(jnp.float32) * value_col).astype(jnp.bfloat16)
     flags = ev_ref[pl.ds(group, 1), :].astype(jnp.float32)
     own = kv.at[z, y, c]
     own[0:half, :] = keys[0:half]
@@ -131,89 +166,7 @@
     own[low_rows : low_rows + half, :] = keys[half:]
     own[low_rows + half :, :] = values[half:]
 
-    pl.semaphore_wait(barrier, 3 + (zs - 1) + (per_group - 1))
-
-    def sized(whole, f, full, low):
-        @pl.when(whole)
-        def _():
-            f(pl.ds(0, full))
-
-        @pl.when(jnp.logical_not(whole))
-        def _():
-            f(pl.ds(0, low))
-
-    def kz_copy(src_z, dst_z, rows):
-        return pltpu.make_async_remote_copy(
-            src_ref=kv.at[z, y, c, rows],
-            dst_ref=kv.at[src_z, y, c, rows],
-            send_sem=kz_send.at[dst_z],
-            recv_sem=kz_recv.at[src_z],
-            device_id=at(dst_z, y, c),
-            device_id_type=MESH,
-        )
-
-    def ky_copy(zi, yi, rows):
-        ref = kv.at[zi, yi, c, rows]
-        return pltpu.make_async_remote_copy(
-            src_ref=ref,
-            dst_ref=ref,
-            send_sem=ky_send.at[zi],
-            recv_sem=ky_recv.at[zi],
-            device_id=y_peer,
-            device_id_type=MESH,
-        )
-
-    def kc_copy(zi, ci, rows):
-        ref = kv.at[zi, :, ci, rows]
-        return pltpu.make_async_remote_copy(
-            src_ref=ref,
-            dst_ref=ref,
-            send_sem=kc_send.at[zi],
-            recv_sem=kc_recv.at[zi],
-            device_id=core_peer,
-            device_id_type=MESH,
-        )
-
-    def send_z(s, carry):
-        zi = turn(s)
-        sized(z >= zi, lambda rows: kz_copy(z, zi, rows).start(), all_rows, low_rows)
-        return carry
-
-    lax.fori_loop(1, zs, send_z, 0)
-
-    def forward_y(s):
-        zi = turn(s)
-
-        def go(rows):
-            @pl.when(zi != z)
-            def _():
-                kz_copy(zi, zi, rows).wait_recv()
-
-            ky_copy(zi, y, rows).start()
-
-        sized(zi >= z, go, all_rows, low_rows)
-
-    def forward_c(s):
-        zi = turn(s)
-
-        def go(rows):
-            ky_copy(zi, 1 - y, rows).wait_recv()
-            kc_copy(zi, c, rows).start()
-
-        sized(zi >= z, go, all_rows, low_rows)
-
-    def ready(s):
-        zi = turn(s)
-        sized(
-            zi >= z,
-            lambda rows: kc_copy(zi, 1 - c, rows).wait_recv(),
-            all_rows,
-            low_rows,
-        )
-
-    forward_y(0)
-
-    for side in range(2):
+    def prepare(side):
         tok = slice(side * half, (side + 1) * half)
 
         def by_head(ref):
@@ -237,6 +190,94 @@
             * LOG2E
         )
         dq_acc[side] = jnp.zeros(dq_acc.shape[1:], jnp.float32)
+
+    pl.semaphore_wait(barrier, 3 + (zs - 1) + (per_group - 1))
+
+    def sized(whole, f, full, low):
+        @pl.when(whole)
+        def _():
+            f(pl.ds(0, full))
+
+        @pl.when(jnp.logical_not(whole))
+        def _():
+            f(pl.ds(0, low))
+
+    def kz_copy(src_z, dst_z, rows):
+        return pltpu.make_async_remote_copy(
+            src_ref=kv.at[z, y, c, rows],
+            dst_ref=kv.at[src_z, y, c, rows],
+            send_sem=kz_send.at[dst_z],
+            recv_sem=kz_recv.at[src_z],
+            device_id=at(dst_z, y, c),
+            device_id_type=MESH,
+        )
+
+    def ky_copy(zi, yi, rows):
+        ref = kv.at[zi, yi, c, rows]
+        return pltpu.make_async_remote_copy(
+            src_ref=ref,
+            dst_ref=ref,
+            send_sem=ky_send.at[zi],
+            recv_sem=ky_recv.at[zi],
+            device_id=y_peer,
+            device_id_type=MESH,
+        )
+
+    def kc_copy(zi, ci, rows):
+        ref = kv.at[zi, :, ci, rows]
+        return pltpu.make_async_remote_copy(
+            src_ref=ref,
+            dst_ref=ref,
+            send_sem=kc_send.at[zi],
+            recv_sem=kc_recv.at[zi],
+            device_id=core_peer,
+            device_id_type=MESH,
+        )
+
+    def send_z(s, carry):
+        zi = turn(s)
+        sized(z >= zi, lambda rows: kz_copy(z, zi, rows).start(), all_rows, low_rows)
+        return carry
+
+    lax.fori_loop(1, zs, send_z, 0)
+
+    def forward_y(s):
+        zi = turn(s)
+
+        def go(rows):
+            @pl.when(zi != z)
+            def _():
+                kz_copy(zi, zi, rows).wait_recv()
+
+            ky_copy(zi, y, rows).start()
+
+        sized(zi >= z, go, all_rows, low_rows)
+
+    def forward_c(s):
+        zi = turn(s)
+
+        def go(rows):
+            ky_copy(zi, 1 - y, rows).wait_recv()
+            kc_copy(zi, c, rows).start()
+
+        sized(zi >= z, go, all_rows, low_rows)
+
+    def ready(s):
+        zi = turn(s)
+        sized(
+            zi >= z,
+            lambda rows: kc_copy(zi, 1 - c, rows).wait_recv(),
+            all_rows,
+            low_rows,
+        )
+
+    forward_y(0)
+    for load in query_loads:
+        load.wait()
+    prepare(1)
+    forward_c(0)
+    forward_y(1)
+    prepare(0)
 
     chunk = 4 * half
     lanes = 2 * half
@@ -312,7 +353,7 @@
 
     def ry_copy(zi, rows):
         return pltpu.make_async_remote_copy(
-            src_ref=part.at[zi, 1 - y, c, rows],
+            src_ref=y_out.at[zi, rows],
             dst_ref=y_in.at[zi, rows],
             send_sem=ry_send.at[zi],
             recv_sem=ry_recv.at[zi],
@@ -322,7 +363,7 @@
 
     def rz_copy(src_z, dst_z, rows):
         return pltpu.make_async_remote_copy(
-            src_ref=part.at[dst_z, y, c, rows],
+            src_ref=z_out.at[dst_z, rows],
             dst_ref=z_in.at[src_z, rows],
             send_sem=rz_send.at[dst_z],
             recv_sem=rz_recv.at[src_z],
@@ -341,6 +382,7 @@
             rc_copy(zi, rows).wait_recv()
             for yi in range(2):
                 part[zi, yi, c, rows, :] += core_in[zi, yi, rows, :]
+            y_out[zi, rows, :] = part[zi, 1 - y, c, rows, :].astype(jnp.bfloat16)
             ry_copy(zi, rows).start()
 
         sized(zi >= z, go, 4 * half, 2 * half)
@@ -350,10 +392,11 @@
 
         def go(rows):
             ry_copy(zi, rows).wait_recv()
-            part[zi, y, c, rows, :] += y_in[zi, rows, :]
+            part[zi, y, c, rows, :] += y_in[zi, rows, :].astype(jnp.float32)
 
             @pl.when(zi != z)
             def _():
+                z_out[zi, rows, :] = part[zi, y, c, rows, :].astype(jnp.bfloat16)
                 rz_copy(z, zi, rows).start()
 
         sized(zi >= z, go, 4 * half, 2 * half)
@@ -362,9 +405,6 @@
         @pl.when(cond)
         def _():
             f(s)
-
-    forward_y(1)
-    forward_c(0)
 
     def step(s, carry):
         when(s + 2 < zs, forward_y, s + 2)
@@ -394,7 +434,7 @@
 
         def go(rows):
             rz_copy(zi, zi, rows).wait_recv()
-            part[z, y, c, rows, :] += z_in[zi, rows, :]
+            part[z, y, c, rows, :] += z_in[zi, rows, :].astype(jnp.float32)
 
         sized(z >= zi, go, 4 * half, 2 * half)
         return carry
@@ -505,14 +545,16 @@
             jax.ShapeDtypeStruct(key_codes.shape, bf16),
             jax.ShapeDtypeStruct(value_codes.shape, bf16),
         ),
-        in_specs=[vmem] * 9,
+        in_specs=[pl.BlockSpec(memory_space=pltpu.HBM)] * 9,
         out_specs=(vmem, vmem, vmem),
         scratch_shapes=[
             pltpu.VMEM((zs, 2, 2, 4 * half + FLAG_ROWS, width), bf16),
             pltpu.VMEM((zs, 2, 2, 4 * half, width), f32),
             pltpu.VMEM((zs, 2, 4 * half, width), f32),
-            pltpu.VMEM((zs, 4 * half, width), f32),
-            pltpu.VMEM((zs, 4 * half, width), f32),
+            pltpu.VMEM((zs, 4 * half, width), bf16),
+            pltpu.VMEM((zs, 4 * half, width), bf16),
+            pltpu.VMEM((zs, 4 * half, width), bf16),
+            pltpu.VMEM((zs, 4 * half, width), bf16),
             pltpu.VMEM((2, side_rows, width), bf16),
             pltpu.VMEM((2, side_rows, width), bf16),
             pltpu.VMEM((2, width, side_rows), bf16),
@@ -526,7 +568,19 @@
         ]
         + [dma((zs,))] * 12
         + [dma((per_group,))] * 2
-        + [dma] * 2,
+        + [dma] * 2
+        + [
+            pltpu.VMEM(queries.shape, bf16),
+            pltpu.VMEM(key_codes.shape[1:], bf16),
+            pltpu.VMEM(key_scale.shape, f32),
+            pltpu.VMEM(value_codes.shape[1:], bf16),
+            pltpu.VMEM(value_scale.shape, f32),
+            pltpu.VMEM(evict_flags.shape, jnp.int32),
+            pltpu.VMEM(out_forward.shape, bf16),
+            pltpu.VMEM(grad_output.shape, bf16),
+            pltpu.VMEM(log_norm.shape, f32),
+            dma((9,)),
+        ],
         compiler_params=pltpu.CompilerParams(
             collective_id=0, has_side_effects=True, vmem_limit_bytes=48 * 2**20
         ),

time: 49.6 us -> 42.4 us (0.85)
  Pallas kernels: 39.4 us -> 32.2 us
    pallas_call x1, Pallas kernels: 39.4 us -> 32.2 us  [local(): pl.pallas_call(functools.partial(kernel, n, head_devices), out_shape=(jax...]
where the time goes in v2:
time: 42.4 us; the launch traced here: 42.1 us
  Pallas kernels  32.2 us (76%)
  local copies, waits for them, and re-layouts  9.2 us (22%)
  between operations  0.66 us (2%)
    pallas_call x1, Pallas kernels, local(): pl.pallas_call(functools.partial(kernel, n, head_devices), out_shape=(jax...  32.2 us
    unnamed x21, local copies, waits for them, and re-layouts  9.2 us

profile of v2, /device:TPU:16, one launch (start us, length us, event | category | flops | bytes accessed | tf_op | source)
XLA Modules:
  0.0 42.1 jit_solution(7611627424656305627)
XLA Ops:
  0.6 0.0 copy-start
  0.6 0.9 %copy-done = bf16[128,1024]{1,0:T(8,128)(2,1)S(1)} copy-done((bf16[128,1024]{1,0:T(8,128)(2,1)S(1)}, bf16[128,1024]{1,0:T(8,128)(2,1)}, u32[]{:S(2)}) %copy-start) | copy-done | bytes 262168
  1.6 0.0 copy-start.1
  1.6 0.9 %copy-done.1 = bf16[128,1024]{1,0:T(8,128)(2,1)S(1)} copy-done((bf16[128,1024]{1,0:T(8,128)(2,1)S(1)}, bf16[128,1024]{1,0:T(8,128)(2,1)}, u32[]{:S(2)}) %copy-start.1) | copy-done | bytes 262168
  2.5 0.0 copy-start.2
  2.5 0.9 %copy-done.2 = bf16[128,1024]{1,0:T(8,128)(2,1)S(1)} copy-done((bf16[128,1024]{1,0:T(8,128)(2,1)S(1)}, bf16[128,1024]{1,0:T(8,128)(2,1)}, u32[]{:S(2)}) %copy-start.2) | copy-done | bytes 262168
  3.5 0.0 copy-start.3
  3.5 0.8 %copy-done.3 = bf16[2,128,128]{2,1,0:T(8,128)(2,1)S(1)} copy-done((bf16[2,128,128]{2,1,0:T(8,128)(2,1)S(1)}, bf16[2,128,128]{2,1,0:T(8,128)(2,1)}, u32[]{:S(2)}) %copy-start.3) | copy-done | bytes 65560
  4.3 0.0 copy-start.4
  4.3 0.8 %copy-done.4 = bf16[2,128,128]{2,1,0:T(8,128)(2,1)S(1)} copy-done((bf16[2,128,128]{2,1,0:T(8,128)(2,1)S(1)}, bf16[2,128,128]{2,1,0:T(8,128)(2,1)}, u32[]{:S(2)}) %copy-start.4) | copy-done | bytes 65560
  5.2 0.0 copy-start.5
  5.2 0.7 %copy-done.5 = f32[8,128]{1,0:T(8,128)S(1)} copy-done((f32[8,128]{1,0:T(8,128)S(1)}, f32[8,128]{1,0:T(8,128)}, u32[]{:S(2)}) %copy-start.5) | copy-done | bytes 4120
  5.9 0.0 copy-start.6
  5.9 0.7 %copy-done.6 = f32[2,128]{1,0:T(2,128)S(1)} copy-done((f32[2,128]{1,0:T(2,128)S(1)}, f32[2,128]{1,0:T(2,128)}, u32[]{:S(2)}) %copy-start.6) | copy-done | bytes 1048
  6.5 0.0 copy-start.7
  6.5 0.7 %copy-done.7 = f32[2,128]{1,0:T(2,128)S(1)} copy-done((f32[2,128]{1,0:T(2,128)S(1)}, f32[2,128]{1,0:T(2,128)}, u32[]{:S(2)}) %copy-start.7) | copy-done | bytes 1048
  7.2 0.0 copy-start.8
  7.2 0.7 %copy-done.8 = s32[2,128]{1,0:T(2,128)S(1)} copy-done((s32[2,128]{1,0:T(2,128)S(1)}, s32[2,128]{1,0:T(2,128)}, u32[]{:S(2)}) %copy-start.8) | copy-done | bytes 1048
  7.9 32.2 %shard_map.112 = (bf16[128,1024]{1,0:T(8,128)(2,1)S(1)}, bf16[2,128,128]{2,1,0:T(8,128)(2,1)S(1)}, bf16[2,128,128]{2,1,0:T(8,128)(2,1)S(1)}) custom-call(bf16[128,1024]{1,0:T(8,128)(2,1)S(1)} %copy-done, bf16[2,128,128]{2,1,0:T(8,128)(2,1)S(1)} %copy-done.3, f32[2,128]{1,0:T(2,128)S(1)} %copy-done.6, bf16[2,128,128]{2,1,0:T(8,128)(2,1)S(1)} %copy-done.4, ...), custom_call_target="tpu_custom_call" | custom-call | tf_op jit(solution)/shard_map/pallas_call | solution.py:541
  40.1 0.7 %copy.15 = bf16[128,1024]{1,0:T(8,128)(2,1)} copy(bf16[128,1024]{1,0:T(8,128)(2,1)S(1)} %get-tuple-element.6) | data formatting | bytes 524288
  40.8 0.6 %copy.16 = bf16[2,128,128]{2,1,0:T(8,128)(2,1)} copy(bf16[2,128,128]{2,1,0:T(8,128)(2,1)S(1)} %get-tuple-element.7) | data formatting | bytes 131072
  41.4 0.6 %copy.17 = bf16[2,128,128]{2,1,0:T(8,128)(2,1)} copy(bf16[2,128,128]{2,1,0:T(8,128)(2,1)S(1)} %get-tuple-element.8) | data formatting | bytes 131072
Async XLA Ops:
  0.6 1.0 %copy-start = (bf16[128,1024]{1,0:T(8,128)(2,1)S(1)}, bf16[128,1024]{1,0:T(8,128)(2,1)}, u32[]{:S(2)}) copy-start(bf16[128,1024]{1,0:T(8,128)(2,1)} %q_hbm.1) | copy-start | bytes 786436
  1.6 0.9 %copy-start.1 = (bf16[128,1024]{1,0:T(8,128)(2,1)S(1)}, bf16[128,1024]{1,0:T(8,128)(2,1)}, u32[]{:S(2)}) copy-start(bf16[128,1024]{1,0:T(8,128)(2,1)} %of_hbm.1) | copy-start | bytes 786436
  2.5 0.9 %copy-start.2 = (bf16[128,1024]{1,0:T(8,128)(2,1)S(1)}, bf16[128,1024]{1,0:T(8,128)(2,1)}, u32[]{:S(2)}) copy-start(bf16[128,1024]{1,0:T(8,128)(2,1)} %go_hbm.1) | copy-start | bytes 786436
  3.5 0.8 %copy-start.3 = (bf16[2,128,128]{2,1,0:T(8,128)(2,1)S(1)}, bf16[2,128,128]{2,1,0:T(8,128)(2,1)}, u32[]{:S(2)}) copy-start(bf16[2,128,128]{2,1,0:T(8,128)(2,1)} %kc_hbm.1) | copy-start | bytes 196612
  4.3 0.8 %copy-start.4 = (bf16[2,128,128]{2,1,0:T(8,128)(2,1)S(1)}, bf16[2,128,128]{2,1,0:T(8,128)(2,1)}, u32[]{:S(2)}) copy-start(bf16[2,128,128]{2,1,0:T(8,128)(2,1)} %vc_hbm.1) | copy-start | bytes 196612
  5.2 0.7 %copy-start.5 = (f32[8,128]{1,0:T(8,128)S(1)}, f32[8,128]{1,0:T(8,128)}, u32[]{:S(2)}) copy-start(f32[8,128]{1,0:T(8,128)} %ln_hbm.1) | copy-start | bytes 12292
  5.9 0.7 %copy-start.6 = (f32[2,128]{1,0:T(2,128)S(1)}, f32[2,128]{1,0:T(2,128)}, u32[]{:S(2)}) copy-start(f32[2,128]{1,0:T(2,128)} %ks_hbm.1) | copy-start | bytes 3076
  6.5 0.7 %copy-start.7 = (f32[2,128]{1,0:T(2,128)S(1)}, f32[2,128]{1,0:T(2,128)}, u32[]{:S(2)}) copy-start(f32[2,128]{1,0:T(2,128)} %vs_hbm.1) | copy-start | bytes 3076
  7.2 0.7 %copy-start.8 = (s32[2,128]{1,0:T(2,128)S(1)}, s32[2,128]{1,0:T(2,128)}, u32[]{:S(2)}) copy-start(s32[2,128]{1,0:T(2,128)} %ev_hbm.1) | copy-start | bytes 3076

commit v3 on v2

--- a/solution.py
+++ b/solution.py
@@ -315,6 +315,14 @@
         evicted = jnp.concatenate(cols, axis=0)
         return jnp.where(evicted == 0.0, 2 * n * half, DELAY)
 
+    def compute_high(zi):
+        k = kv[zi, :, :, low_rows : low_rows + half, :].reshape(chunk, width)
+        v = kv[zi, :, :, low_rows + half :, :].reshape(chunk, width)
+        key_pos = (2 * n - 1 - zi * 4 - row_block) * half + row_in
+        dk, dv = terms(k, v, jnp.transpose(k), key_pos, limits(zi, half), 1)
+        part[zi, :, :, 2 * half : 3 * half, :] = dk
+        part[zi, :, :, 3 * half :, :] = dv
+
     def compute(s):
         zi = turn(s)
         k = kv[zi, :, :, 0:half, :].reshape(chunk, width)
@@ -332,14 +340,9 @@
             part[zi, :, :, 0:half, :] += dk
             part[zi, :, :, half : 2 * half, :] += dv
 
-        @pl.when(zi >= z)
+        @pl.when(zi > z)
         def _():
-            k = kv[zi, :, :, low_rows : low_rows + half, :].reshape(chunk, width)
-            v = kv[zi, :, :, low_rows + half :, :].reshape(chunk, width)
-            key_pos = (2 * n - 1 - zi * 4 - row_block) * half + row_in
-            dk, dv = terms(k, v, jnp.transpose(k), key_pos, limits(zi, half), 1)
-            part[zi, :, :, 2 * half : 3 * half, :] = dk
-            part[zi, :, :, 3 * half :, :] = dv
+            compute_high(zi)
 
     def rc_copy(zi, rows):
         return pltpu.make_async_remote_copy(
@@ -411,16 +414,21 @@
         when(s + 1 < zs, forward_c, s + 1)
         ready(s)
         compute(s)
-        reduce_c(s)
-        when(s >= 1, reduce_y, s - 1)
-        when(s >= 2, reduce_z, s - 2)
+        when(s >= 1, reduce_c, s)
+        when(s >= 2, reduce_y, s - 1)
+        when(s >= 3, reduce_z, s - 2)
         return carry
 
     lax.fori_loop(0, zs, step, 0)
-    reduce_y(zs - 1)
+    compute_high(z)
+    reduce_c(0)
     if zs >= 2:
+        reduce_y(zs - 1)
+    if zs >= 3:
         reduce_z(zs - 2)
-    reduce_z(zs - 1)
+    reduce_y(0)
+    if zs >= 2:
+        reduce_z(zs - 1)
 
     for side in range(2):
         dq = jnp.transpose(dq_acc[side]).astype(jnp.bfloat16)
@@ -428,6 +436,8 @@
             dq_ref[side * half : (side + 1) * half, h * width : (h + 1) * width] = dq[
                 h * half : (h + 1) * half
             ]
+
+    reduce_z(0)
 
     def collect(s, carry):
         zi = turn(s)
@@ -513,6 +523,25 @@
     lax.fori_loop(0, zs, sent, 0)
     h_copy.wait()
     put(1 - group, head_in)
+
+
+def place(dq, dk, dv, dq_out, dk_out, dv_out, dq_vmem, dk_vmem, dv_vmem, in_sems, out_sems):
+    held = (dq_vmem, dk_vmem, dv_vmem)
+    loads = [
+        pltpu.make_async_copy(src, dst, in_sems.at[i])
+        for i, (src, dst) in enumerate(zip((dq, dk, dv), held))
+    ]
+    stores = [
+        pltpu.make_async_copy(src, dst, out_sems.at[i])
+        for i, (src, dst) in enumerate(zip(held, (dq_out, dk_out, dv_out)))
+    ]
+    for load in loads:
+        load.start()
+    for load, store in zip(loads, stores):
+        load.wait()
+        store.start()
+    for store in stores:
+        store.wait()
 
 
 def local(
@@ -538,7 +567,7 @@
     f32, bf16 = jnp.float32, jnp.bfloat16
     vmem = pl.BlockSpec(memory_space=pltpu.VMEM)
     dma = pltpu.SemaphoreType.DMA
-    return pl.pallas_call(
+    grads = pl.pallas_call(
         functools.partial(kernel, n, head_devices),
         out_shape=(
             jax.ShapeDtypeStruct(queries.shape, bf16),
@@ -582,7 +611,7 @@
             dma((9,)),
         ],
         compiler_params=pltpu.CompilerParams(
-            collective_id=0, has_side_effects=True, vmem_limit_bytes=48 * 2**20
+            collective_id=0, has_side_effects=True, vmem_limit_bytes=62 * 2**20
         ),
     )(
         queries,
@@ -595,6 +624,14 @@
         grad_output,
         log_norm,
     )
+    anywhere = pl.BlockSpec(memory_space=pl.ANY)
+    return pl.pallas_call(
+        place,
+        out_shape=tuple(jax.ShapeDtypeStruct(g.shape, g.dtype) for g in grads),
+        in_specs=[anywhere] * 3,
+        out_specs=(anywhere,) * 3,
+        scratch_shapes=[pltpu.VMEM(g.shape, g.dtype) for g in grads] + [dma((3,))] * 2,
+    )(*grads)
 
 
 def solution(mesh):

time: 42.4 us -> 34.9 us (0.82)
  local copies, waits for them, and re-layouts: 9.2 us -> 0 us
  Pallas kernels: 32.2 us -> 34 us
    unnamed x21 -> x0, local copies, waits for them, and re-layouts: 9.2 us -> none
    pallas_call x0 -> x1, Pallas kernels: none -> 1.74 us  [local(): pl.pallas_call(place, out_shape=tuple((jax.ShapeDtypeStruct(g.shape, g.dt...]
where the time goes in v3:
time: 34.9 us; the launch traced here: 34.6 us
  Pallas kernels  34 us (97%)
  between operations  0.64 us (2%)
    pallas_call x1, Pallas kernels, local(): pl.pallas_call(functools.partial(kernel, n, head_devices), out_shape=(jax...  32.2 us
    pallas_call x1, Pallas kernels, local(): pl.pallas_call(place, out_shape=tuple((jax.ShapeDtypeStruct(g.shape, g.dt...  1.74 us

profile of v3, /device:TPU:16, one launch (start us, length us, event | category | flops | bytes accessed | tf_op | source)
XLA Modules:
  0.0 34.6 jit_solution(8142289863580546641)
XLA Ops:
  0.6 32.2 %shard_map.112 = (bf16[128,1024]{1,0:T(8,128)(2,1)}, bf16[2,128,128]{2,1,0:T(8,128)(2,1)}, bf16[2,128,128]{2,1,0:T(8,128)(2,1)}) custom-call(bf16[128,1024]{1,0:T(8,128)(2,1)} %q_hbm.1, bf16[2,128,128]{2,1,0:T(8,128)(2,1)} %kc_hbm.1, f32[2,128]{1,0:T(2,128)} %ks_hbm.1, bf16[2,128,128]{2,1,0:T(8,128)(2,1)} %vc_hbm.1, f32[2,128]{1,0:T(2,128)} %vs_hbm.1, ...), custom_call_target="tpu_custom_call" | custom-call | tf_op jit(solution)/shard_map/pallas_call | solution.py:570
  32.9 1.7 %shard_map.113 = (bf16[128,1024]{1,0:T(8,128)(2,1)}, bf16[2,128,128]{2,1,0:T(8,128)(2,1)}, bf16[2,128,128]{2,1,0:T(8,128)(2,1)}) custom-call(bf16[128,1024]{1,0:T(8,128)(2,1)} %get-tuple-element.6.dq, bf16[2,128,128]{2,1,0:T(8,128)(2,1)} %get-tuple-element.7.dk, bf16[2,128,128]{2,1,0:T(8,128)(2,1)} %get-tuple-element.8.dv), custom_call_target="tpu_custom_call" | custom-call | tf_op jit(solution)/shard_map/pallas_call | solution.py:628
